TPU v7x, 32 devices: a whole 2x2x4 slice. The times are simulated.
32 devices in a mesh: mem: 2 (over x), tile: 4 (over z), lev: 4 (over y, core).
Axes of the slice: x: 2, y: 2, z: 4, core: 2. Of those that a mesh axis runs over, the one named last changes fastest.
Arguments:
- ensemble: bfloat16 [32, 2, 64, 32768], P(('mem', 'tile'), None, 'lev'), may hold values from -6 to 6
- alpha: bfloat16 [20, 32, 32768], P('lev', ('mem', 'tile')), may hold values from -6 to 6
- vert_root: bfloat16 [64, 20], P('lev'), may hold values from -1.25 to 1.25
- cotangent: bfloat16 [2, 64, 32768], P('mem', 'lev', 'tile'), may hold values from -6 to 6
Outputs:
- increment: bfloat16 [2, 64, 32768], P('mem', 'lev', 'tile')
- alpha_grad: bfloat16 [20, 32, 32768], P('lev', ('mem', 'tile'))
All inputs are finite; a program needn't handle non-finite values.
Results may differ from a plain program's by a relative error of at most 0.008.
Values may be sent and summed in bfloat16 or wider, within the bound.
A program may use at most 128 MiB of HBM per device.

v0:
```python
import math

import jax
import jax.numpy as jnp
from jax import lax
from jax.sharding import PartitionSpec as P

MEMBERS = 32


def lift_control(alpha, vert_root):
    modes_all = lax.all_gather(alpha, "lev", axis=0, tiled=True)
    return jnp.einsum(
        "lm,mkg->klg", vert_root, modes_all, preferred_element_type=jnp.float32
    ).astype(jnp.bfloat16)


def level_adjoint(vert_root, cross_back, scale):
    gathered_sum = lax.psum_scatter(
        jnp.einsum("lm,klg->mkg", vert_root, cross_back, preferred_element_type=jnp.float32),
        "lev",
        scatter_dimension=0,
        tiled=True,
    )
    return (gathered_sum * scale).astype(jnp.bfloat16)


def on_device(ensemble, alpha, vert_root, cotangent):
    scale = 1.0 / math.sqrt(MEMBERS - 1)
    var_cot = lax.all_gather(cotangent, "mem", axis=0, tiled=True)
    lifted = lift_control(alpha, vert_root)
    partial_all = jnp.einsum("kvlg,klg->vlg", ensemble, lifted, preferred_element_type=jnp.float32)
    partial_value = lax.psum_scatter(partial_all, "tile", scatter_dimension=2, tiled=True)
    full_cot = lax.all_gather(var_cot, "tile", axis=2, tiled=True)
    cross = jnp.einsum(
        "kvlg,vlg->klg", ensemble, full_cot, preferred_element_type=jnp.float32
    ).astype(jnp.bfloat16)
    summed = lax.psum_scatter(partial_value, "mem", scatter_dimension=0, tiled=True)
    finished = (summed * scale).astype(jnp.bfloat16)
    alpha_grad = level_adjoint(vert_root, cross, scale)
    return (finished, alpha_grad)


def solution(mesh):
    in_specs = (
        P(("mem", "tile"), None, "lev", None),
        P("lev", ("mem", "tile"), None),
        P("lev", None),
        P("mem", "lev", "tile"),
    )
    out_specs = (P("mem", "lev", "tile"), P("lev", ("mem", "tile"), None))
    return jax.shard_map(
        on_device, mesh=mesh, in_specs=in_specs, out_specs=out_specs, check_vma=False
    )
```

profile of v0, /device:TPU:0, one launch (start us, length us, event | category | flops | bytes accessed | tf_op | source)
XLA Modules:
  0.0 398.9 jit_solution(4775599221622574871)
XLA Ops:
  7.2 0.0 copy-start
  7.2 0.0 all-gather.3.cloned.1.call-start
  7.2 0.7 all-gather.3.cloned.1.call-update
  7.9 0.0 all-gather.5.cloned.1.call-start
  8.0 13.2 %all_gather.10 = bf16[2,16,8192]{2,1,0:T(8,128)(2,1)} all-gather(bf16[1,16,8192]{2,1,0:T(8,128)(2,1)} %param.7), channel_id=1, replica_groups=mesh['mem'=2,'tile'=4,'lev'=4] {'mem'}, dimensions={0}, use_global_device_ids=true | all-gather | bytes 786432 | tf_op jit(solution)/shard_map/all_gather | solution.py:30
  21.1 0.0 all-gather.5.cloned.1.call-update
  21.1 0.0 reduce-scatter.3.cloned.1.call-start
  21.2 31.6 %all-gather.3.cloned.1.call-done = bf16[20,4,32768]{2,1,0:T(4,128)(2,1)} async-done(((bf16[5,4,32768]{2,1,0:T(4,128)(2,1)}), bf16[20,4,32768]{2,1,0:T(4,128)(2,1)}) %all-gather.3.cloned.1.call-update) | async-done | bytes 5242896 | tf_op jit(solution)/shard_map/all_gather | solution.py:12
  52.7 0.0 copy-done
  52.7 5.7 %fusion.1 = f32[16,32768,4]{1,0,2:T(8,128)S(1)} fusion(bf16[20,4,32768]{2,1,0:T(4,128)(2,1)} %all-gather.3.cloned.1.call-done, bf16[16,20]{1,0:T(8,128)(2,1)S(1)} %copy-done), kind=kOutput, calls=%fused_computation.3 | convolution fusion | flops 88080384 | bytes 13632128 | tf_op jit(solution)/shard_map/lm,mkg->klg/dot_general | solution.py:13
  58.4 7.5 %multiply_reduce_fusion.1 = f32[16,32768,2]{1,0,2:T(8,128)} fusion(f32[16,32768,4]{1,0,2:T(8,128)S(1)} %fusion.1, bf16[4,2,16,32768]{3,2,1,0:T(8,128)(2,1)} %param.4), kind=kLoop, calls=%fused_computation.5 | loop fusion | flops 11534336 | bytes 20971520 | tf_op jit(solution)/shard_map/kvlg,klg->vlg/dot_general | solution.py:32
  65.9 0.0 reduce-scatter.3.cloned.1.call-update
  66.0 0.0 all-reduce.3.cloned.1.call-start
  66.0 34.3 %all-gather.5.cloned.1.call-done = bf16[2,16,32768]{2,1,0:T(8,128)(2,1)} async-done(((bf16[2,16,8192]{2,1,0:T(8,128)(2,1)}), bf16[2,16,32768]{2,1,0:T(8,128)(2,1)}) %all-gather.5.cloned.1.call-update) | async-done | bytes 2097168 | tf_op jit(solution)/shard_map/all_gather | solution.py:34
  100.3 3.8 bitcast_convert_fusion
  104.1 11.0 %multiply_reduce_fusion = bf16[16,32768,4]{1,0,2:T(8,128)(2,1)} fusion(f32[16,32768,2]{1,0,2:T(8,128)} %bitcast_convert_fusion, bf16[4,2,16,32768]{3,2,1,0:T(8,128)(2,1)} %param.4), kind=kLoop, calls=%fused_computation.4 | loop fusion | flops 10485760 | bytes 16777216 | tf_op jit(solution)/shard_map/kvlg,vlg->klg/dot_general | solution.py:35
  115.0 4.2 %convolution_bitcast_fusion = f32[20,4,32768]{2,0,1:T(8,128)S(1)} fusion(bf16[16,32768,4]{1,0,2:T(8,128)(2,1)} %multiply_reduce_fusion, bf16[16,20]{1,0:T(8,128)(2,1)S(1)} %copy-done), kind=kOutput, calls=%fused_computation | convolution fusion | flops 83886080 | bytes 14680704 | tf_op jit(solution)/shard_map/lm,klg->mkg/dot_general | solution.py:20
  119.2 7.8 %copy.9 = f32[20,4,32768]{2,1,0:T(4,128)} copy(f32[20,4,32768]{2,0,1:T(8,128)S(1)} %convolution_bitcast_fusion) | data formatting | bytes 20971520 | tf_op jit(solution)/shard_map/lm,klg->mkg/dot_general | solution.py:20
  127.1 0.0 copy-start.1
  127.1 0.0 all-reduce.3.cloned.1.call-update
  127.1 0.0 reduce-scatter.5.cloned.1.call-start
  127.1 0.6 copy-done.1
  127.7 0.6 dynamic-slice
  129.0 49.1 %reduce-scatter.3.cloned.1.call-done = f32[2,16,8192]{2,1,0:T(8,128)} async-done(((f32[2,16,32768]{2,1,0:T(8,128)}), f32[2,16,8192]{2,1,0:T(8,128)}) %reduce-scatter.3.cloned.1.call-update) | async-done | bytes 1048592 | tf_op jit(solution)/shard_map/reduce_scatter | solution.py:33
  178.1 0.0 reduce-scatter.5.cloned.1.call-update
  178.1 189.8 %all-reduce.3.cloned.1.call-done = f32[20,4,32768]{2,1,0:T(4,128)} async-done(((f32[20,4,32768]{2,1,0:T(4,128)}), f32[20,4,32768]{2,1,0:T(4,128)}) %all-reduce.3.cloned.1.call-update) | async-done | bytes 10485776
  367.9 3.5 fusion.5
  371.4 19.2 %reduce-scatter.5.cloned.1.call-done = f32[1,16,8192]{2,1,0:T(8,128)} async-done(((f32[2,16,8192]{2,1,0:T(8,128)}), f32[1,16,8192]{2,1,0:T(8,128)}) %reduce-scatter.5.cloned.1.call-update) | async-done | bytes 524304 | tf_op jit(solution)/shard_map/reduce_scatter | solution.py:38
  390.6 1.8 multiply_convert_fusion
Async XLA Ops:
  7.2 45.6 %copy-start = (bf16[16,20]{1,0:T(8,128)(2,1)S(1)}, bf16[16,20]{1,0:T(8,128)(2,1)}, u32[]{:S(2)}) copy-start(bf16[16,20]{1,0:T(8,128)(2,1)} %param.6) | copy-start | bytes 1924
  7.2 45.6 %all-gather.3.cloned.1.call-start = ((), (), s32[]{:S(2)}) async-start(), calls=%async_computation.2 | async-start | bytes 6553600 | tf_op jit(solution)/shard_map/all_gather | solution.py:12
  7.9 92.4 %all-gather.5.cloned.1.call-start = ((), (), s32[]{:S(2)}) async-start(), calls=%async_computation.5 | async-start | bytes 2621440 | tf_op jit(solution)/shard_map/all_gather | solution.py:34
  21.1 157.0 %reduce-scatter.3.cloned.1.call-start = ((), (), s32[]{:S(2)}) async-start(), calls=%async_computation.3 | async-start | bytes 5242880 | tf_op jit(solution)/shard_map/reduce_scatter | solution.py:33
  66.0 301.9 %all-reduce.3.cloned.1.call-start = ((), (), s32[]{:S(2)}) async-start(), calls=%async_computation.6 | async-start | bytes 20971520
  127.1 0.7 copy-start.1
  127.1 263.5 %reduce-scatter.5.cloned.1.call-start = ((), (), s32[]{:S(2)}) async-start(), calls=%async_computation.4 | async-start | bytes 1572864 | tf_op jit(solution)/shard_map/reduce_scatter | solution.py:38
Sparse Core Ops, SparseCore 0:
  9.6 43.1 all-gather.2
  54.3 45.9 all-gather.4
  102.6 75.4 reduce-scatter.2
  180.6 187.2 all-reduce.2
  370.1 20.4 reduce-scatter.4
where the time goes:
time: 399 us
  waiting for transfers between devices  325 us (81%)
  other arithmetic  27.5 us (7%)
  between operations  14.5 us (4%)
  blocking collectives  13.2 us (3%)
  matrix products  9.86 us (2%)
  local copies, waits for them, and re-layouts  9 us (2%)
    unnamed x6, waiting for transfers between devices  191 us
    reduce_scatter x1, waiting for transfers between devices, on_device(): lax.psum_scatter(partial_all, 'tile', scatter_dimension=2, tiled=True)  49.1 us
    all_gather x1, waiting for transfers between devices, on_device(): full_cot = lax.all_gather(var_cot, 'tile', axis=2, tiled=True)  34.3 us
    all_gather x1, waiting for transfers between devices, lift_control(): modes_all = lax.all_gather(alpha, 'lev', axis=0, tiled=True)  31.6 us
    reduce_scatter x1, waiting for transfers between devices, on_device(): lax.psum_scatter(partial_value, 'mem', scatter_dimension=0, tiled=True)  19.2 us
    all_gather x1, blocking collectives, on_device(): var_cot = lax.all_gather(cotangent, 'mem', axis=0, tiled=True)  13.2 us
    dot_general x1, other arithmetic, on_device(): jnp.einsum('kvlg,vlg->klg', ensemble, full_cot, preferred_element_type=jn...  11 us
  transfers between devices with their start and end apart: 5, of which 5 were waited for; matrix products, arithmetic and copies ran while one was open for 11% of the time, Pallas kernels for 0%

commit v1 on v0

v1 whole, which is shorter than its diff:
```python
import functools
import math

import jax
import jax.numpy as jnp
from jax import lax
from jax.experimental import pallas as pl
from jax.experimental.pallas import tpu as pltpu
from jax.sharding import PartitionSpec as P

MEMBERS = 32
MESH = pl.DeviceIdType.MESH
F32 = jnp.float32
BF16 = jnp.bfloat16

CHUNKS = 8
AHEAD = 3
SLOTS = 4
WIDE = 256


def kernel(scale, tiles, levels, ens_ref, alpha_ref, root_ref, cot_ref, inc_ref, grad_ref,
           ens, alpha, cot, lift_w, back_w, keep_c, keep_own, keep_y,
           c1s, c1r, c2s, c2r, d1s, d1r, d2s, d2r,
           ens_sem, own_sem, cot_sem, a_ss, a_rs, bt_ss, bt_rs, bm_ss, bm_rs,
           c1_ss, c1_rs, c2_ss, c2_rs, d1_ss, d1_rs, d2_ss, d2_rs):
    chunks, rows, width = alpha_ref.shape
    members = ens_ref.shape[0]
    modes = root_ref.shape[1] // 4
    pairs = members * tiles
    cells = chunks * width
    mem, tile, lev = lax.axis_index("mem"), lax.axis_index("tile"), lax.axis_index("lev")
    near = {"lev": lev + 1 - 2 * (lev % 2)}
    far = {"lev": (lev + 2) % 4}
    twin = {"mem": 1 - mem}
    tile_to = [{"tile": (tile + i) % tiles} for i in range(tiles)]
    tile_from = [(tile + tiles - i) % tiles for i in range(tiles)]

    def remote(src, dst, ss, rs, to):
        return pltpu.make_async_remote_copy(
            src_ref=src, dst_ref=dst, send_sem=ss, recv_sem=rs, device_id=to, device_id_type=MESH
        )

    def a_far(c):
        return remote(alpha_ref.at[c], alpha.at[c, 2], a_ss.at[c, 0], a_rs.at[c, 0], far)

    def a_near(c):
        return remote(alpha_ref.at[c], alpha.at[c, 1], a_ss.at[c, 1], a_rs.at[c, 1], near)

    def a_pass(c):
        return remote(alpha.at[c, 2], alpha.at[c, 3], a_ss.at[c, 2], a_rs.at[c, 2], near)

    def a_own(c):
        return pltpu.make_async_copy(alpha_ref.at[c], alpha.at[c, 0], own_sem.at[c])

    def b_own(c):
        return pltpu.make_async_copy(cot_ref.at[c], cot.at[c, 0, tile], cot_sem.at[c])

    def b_tile(c, i):
        return remote(cot_ref.at[c], cot.at[c, 0, tile], bt_ss.at[c, i], bt_rs.at[c, i], tile_to[i])

    def b_twin(c, i):
        src = cot_ref.at[c] if i == 0 else cot.at[c, 0, tile_from[i]]
        return remote(src, cot.at[c, 1, tile_from[i]], bm_ss.at[c, i], bm_rs.at[c, i], twin)

    def c_twin(c):
        return remote(c1s.at[c], c1r.at[c], c1_ss.at[c], c1_rs.at[c], twin)

    def c_tile(c, i):
        src = c2s.at[c, (tile + i) % tiles]
        return remote(src, c2r.at[c, i - 1], c2_ss.at[c, i], c2_rs.at[c, i], tile_to[i])

    def d_near(c):
        return remote(d1s.at[c], d1r.at[c], d1_ss.at[c], d1_rs.at[c], near)

    def d_far(c):
        return remote(d2s.at[c], d2r.at[c], d2_ss.at[c], d2_rs.at[c], far)

    def e_load(c, t):
        src = ens_ref.at[:, :, :, pl.ds(pl.multiple_of(t * cells + c * width, width), width)]
        return pltpu.make_async_copy(src, ens.at[c % SLOTS, t], ens_sem.at[c % SLOTS, t])

    def first_sends(c):
        a_far(c).start()
        for i in range(1, tiles):
            b_tile(c, i).start()
        b_twin(c, 0).start()
        a_near(c).start()
        a_own(c).start()
        b_own(c).start()

    barrier = pltpu.get_barrier_semaphore()
    greeted = [near, far, twin] + tile_to[1:]
    for other in greeted:
        pl.semaphore_signal(barrier, inc=1, device_id=other, device_id_type=MESH)
    for c in range(min(2, chunks)):
        for t in range(tiles):
            e_load(c, t).start()
    pl.semaphore_wait(barrier, len(greeted))

    @pl.loop(0, min(AHEAD, chunks))
    def _(c):
        first_sends(c)

    def mode_of(j):
        r = jnp.where(j >= modes, 1, 0) + jnp.where(j >= 2 * modes, 1, 0) + jnp.where(j >= 3 * modes, 1, 0)
        home = jnp.where(
            r == 0, lev, jnp.where(r == 1, near["lev"], jnp.where(r == 2, far["lev"], 3 - lev))
        )
        return home * modes + (j - r * modes)

    def hot(mask):
        return jnp.where(mask, 1.0, 0.0).astype(BF16)

    def iota(shape, axis):
        return lax.broadcasted_iota(jnp.int32, shape, axis)

    high, deep = pairs * levels, 4 * rows
    root = root_ref[...]
    by_level = hot(iota((high, levels), 0) % levels == iota((high, levels), 1))
    by_mode = hot(mode_of(iota((4 * modes, deep), 1) // pairs) == iota((4 * modes, deep), 0))
    spread = jnp.dot(by_level, root, preferred_element_type=F32).astype(BF16)
    spread = jnp.dot(spread, by_mode, preferred_element_type=F32)
    same = iota((high, deep), 0) // levels == iota((high, deep), 1) % pairs
    lift_w[...] = jnp.where(same, spread, 0.0).astype(BF16)
    by_mode_t = hot(mode_of(iota((deep, 4 * modes), 0) // pairs) == iota((deep, 4 * modes), 1))
    by_level_t = hot(iota((levels, high), 1) % levels == iota((levels, high), 0))
    spread_t = lax.dot_general(
        by_mode_t, root, (((1,), (1,)), ((), ())), preferred_element_type=F32
    ).astype(BF16)
    spread_t = jnp.dot(spread_t, by_level_t, preferred_element_type=F32)
    same_t = iota((deep, high), 1) // levels == iota((deep, high), 0) % pairs
    back_w[...] = jnp.where(same_t, spread_t, 0.0).astype(BF16)

    def compute_adjoint(c):
        e, slot = c % SLOTS, c % SLOTS

        @pl.loop(0, width // WIDE)
        def _(j):
            cols = pl.ds(pl.multiple_of(j * WIDE, WIDE), WIDE)
            own = [cot[c, 0, t, :, cols].astype(F32) for t in range(tiles)]
            other = [cot[c, 1, t, :, cols].astype(F32) for t in range(tiles)]
            cross = jnp.concatenate(
                [
                    (
                        ens[e, t, k, mem, :, cols].astype(F32) * own[t]
                        + ens[e, t, k, 1 - mem, :, cols].astype(F32) * other[t]
                    ).astype(BF16)
                    for k in range(members)
                    for t in range(tiles)
                ],
                axis=0,
            )
            back = jnp.dot(back_w[...], cross, preferred_element_type=F32)
            keep_own[slot, :, cols] = back[:rows]
            d1s[c, 0, :, cols] = back[rows : 2 * rows].astype(BF16)
            keep_y[slot, :, cols] = back[2 * rows : 3 * rows]
            d1s[c, 1, :, cols] = back[3 * rows :].astype(BF16)

    def compute_lift(c):
        e, slot = c % SLOTS, c % SLOTS

        @pl.loop(0, width // WIDE)
        def _(j):
            cols = pl.ds(pl.multiple_of(j * WIDE, WIDE), WIDE)
            fields = alpha[c, :, :, cols].reshape(deep, WIDE)
            lifted = jnp.dot(lift_w[...], fields, preferred_element_type=F32)
            lifted = lifted.astype(BF16).astype(F32)
            for t in range(tiles):
                own = other = None
                for k in range(members):
                    at = (k * tiles + t) * levels
                    part = lifted[at : at + levels]
                    one = ens[e, t, k, mem, :, cols].astype(F32) * part
                    two = ens[e, t, k, 1 - mem, :, cols].astype(F32) * part
                    own = one if own is None else own + one
                    other = two if other is None else other + two
                keep_c[slot, t, :, cols] = own
                c1s[c, t, :, cols] = other.astype(BF16)

    @pl.loop(0, chunks + 3)
    def _(step):
        @pl.when(step < chunks)
        def _():
            c = step

            @pl.when(c + AHEAD < chunks)
            def _():
                first_sends(c + AHEAD)

            @pl.when(c + 2 < chunks)
            def _():
                for t in range(tiles):
                    e_load(c + 2, t).start()

            for i in range(1, tiles):
                b_tile(c, i).wait_recv()
                b_twin(c, i).start()
            a_far(c).wait_recv()
            a_pass(c).start()

        @pl.when((step >= 1) & (step <= chunks))
        def _():
            c = step - 1
            for t in range(tiles):
                e_load(c, t).wait()
            b_own(c).wait()
            for i in range(tiles):
                b_twin(c, i).wait_recv()
            compute_adjoint(c)
            d_near(c).start()
            a_own(c).wait()
            a_near(c).wait_recv()
            a_pass(c).wait_recv()
            compute_lift(c)
            c_twin(c).start()
            d_near(c).wait_recv()
            slot = c % SLOTS
            d2s[c] = (keep_y[slot] + d1r[c, 1].astype(F32)).astype(BF16)
            d_far(c).start()
            keep_own[slot] = keep_own[slot] + d1r[c, 0].astype(F32)

        @pl.when((step >= 2) & (step <= chunks + 1))
        def _():
            c = step - 2
            slot = c % SLOTS
            c_twin(c).wait_recv()
            for t in range(tiles):
                total = keep_c[slot, t] + c1r[c, t].astype(F32)
                keep_c[slot, t] = total
                c2s[c, t] = total.astype(BF16)
            for i in range(1, tiles):
                c_tile(c, i).start()

        @pl.when(step >= 3)
        def _():
            c = step - 3
            slot = c % SLOTS
            total = keep_c[slot, tile]
            for i in range(1, tiles):
                c_tile(c, i).wait_recv()
                total = total + c2r[c, i - 1].astype(F32)
            inc_ref[:, pl.ds(pl.multiple_of(c * width, width), width)] = (total * scale).astype(BF16)
            d_far(c).wait_recv()
            grad_ref[c] = ((keep_own[slot] + d2r[c].astype(F32)) * scale).astype(BF16)

    @pl.loop(0, chunks)
    def _(c):
        a_far(c).wait_send()
        a_near(c).wait_send()
        a_pass(c).wait_send()
        b_twin(c, 0).wait_send()
        for i in range(1, tiles):
            b_tile(c, i).wait_send()
            b_twin(c, i).wait_send()
            c_tile(c, i).wait_send()
        c_twin(c).wait_send()
        d_near(c).wait_send()
        d_far(c).wait_send()


def on_device(tiles, ensemble, alpha, vert_root, cotangent):
    scale = 1.0 / math.sqrt(MEMBERS - 1)
    members, _, levels, whole = ensemble.shape
    modes = alpha.shape[0]
    cells = whole // tiles
    chunks, width = CHUNKS, cells // CHUNKS
    rows = modes * members * tiles
    packed = alpha.reshape(modes, members, tiles, chunks, width)
    packed = packed.transpose(3, 0, 1, 2, 4).reshape(chunks, rows, width)
    cot = cotangent.reshape(levels, chunks, width).transpose(1, 0, 2)
    vmem, dma = pltpu.VMEM, pltpu.SemaphoreType.DMA
    sums = (chunks, tiles, levels, width)
    increment, grad = pl.pallas_call(
        functools.partial(kernel, scale, tiles, levels),
        out_shape=(
            jax.ShapeDtypeStruct((levels, cells), BF16),
            jax.ShapeDtypeStruct((chunks, rows, width), BF16),
        ),
        in_specs=[
            pl.BlockSpec(memory_space=pl.ANY),
            pl.BlockSpec(memory_space=pl.ANY),
            pl.BlockSpec(memory_space=pltpu.VMEM),
            pl.BlockSpec(memory_space=pl.ANY),
        ],
        out_specs=(pl.BlockSpec(memory_space=pltpu.VMEM), pl.BlockSpec(memory_space=pltpu.VMEM)),
        scratch_shapes=[
            vmem((SLOTS, tiles, members, 2, levels, width), BF16),
            vmem((chunks, 4, rows, width), BF16),
            vmem((chunks, 2, tiles, levels, width), BF16),
            vmem((members * tiles * levels, 4 * rows), BF16),
            vmem((4 * rows, members * tiles * levels), BF16),
            vmem((SLOTS, tiles, levels, width), F32),
            vmem((SLOTS, rows, width), F32),
            vmem((SLOTS, rows, width), F32),
            vmem(sums, BF16),
            vmem(sums, BF16),
            vmem(sums, BF16),
            vmem((chunks, tiles - 1, levels, width), BF16),
            vmem((chunks, 2, rows, width), BF16),
            vmem((chunks, 2, rows, width), BF16),
            vmem((chunks, rows, width), BF16),
            vmem((chunks, rows, width), BF16),
            dma((SLOTS, tiles)),
            dma((chunks,)),
            dma((chunks,)),
            dma((chunks, 3)),
            dma((chunks, 3)),
            dma((chunks, tiles)),
            dma((chunks, tiles)),
            dma((chunks, tiles)),
            dma((chunks, tiles)),
            dma((chunks,)),
            dma((chunks,)),
            dma((chunks, tiles)),
            dma((chunks, tiles)),
            dma((chunks,)),
            dma((chunks,)),
            dma((chunks,)),
            dma((chunks,)),
        ],
        compiler_params=pltpu.CompilerParams(
            collective_id=0, has_side_effects=True, vmem_limit_bytes=60 * 1024 * 1024
        ),
    )(ensemble, packed, vert_root, cot)
    grad = grad.reshape(chunks, modes, members, tiles, width).transpose(1, 2, 3, 0, 4)
    return increment[None], grad.reshape(modes, members, whole)


def solution(mesh):
    in_specs = (
        P(("mem", "tile"), None, "lev", None),
        P("lev", ("mem", "tile"), None),
        P("lev", None),
        P("mem", "lev", "tile"),
    )
    out_specs = (P("mem", "lev", "tile"), P("lev", ("mem", "tile"), None))
    return jax.shard_map(
        functools.partial(on_device, mesh.shape["tile"]),
        mesh=mesh, in_specs=in_specs, out_specs=out_specs, check_vma=False,
    )
```

time: 399 us -> 83.2 us (0.21)
  waiting for transfers between devices: 325 us -> 0 us
  Pallas kernels: 0 us -> 68.9 us
  other arithmetic: 27.5 us -> 0 us
  between operations: 14.5 us -> 0.68 us
  blocking collectives: 13.2 us -> 0 us
  matrix products: 9.86 us -> 0 us
  local copies, waits for them, and re-layouts: 9 us -> 13.3 us
    unnamed x6 -> x0, waiting for transfers between devices: 191 us -> none
    pallas_call x0 -> x1, Pallas kernels: none -> 68.9 us  [on_device(): pl.pallas_call(functools.partial(kernel, scale, tiles, levels), out_shape...]
    reduce_scatter x2 -> x0, waiting for transfers between devices: 68.4 us -> none  [the longest x1 49.1 us: on_device(): lax.psum_scatter(partial_all, 'tile', scatter_dimension=2, tiled=True)]
    all_gather x2 -> x0, waiting for transfers between devices: 65.8 us -> none  [the longest x1 34.3 us: on_device(): full_cot = lax.all_gather(var_cot, 'tile', axis=2, tiled=True)]
    dot_general x2 -> x0, other arithmetic: 18.5 us -> none  [the longest x1 11 us: on_device(): jnp.einsum('kvlg,vlg->klg', ensemble, full_cot, preferred_element_type=jn...]
    all_gather x1 -> x0, blocking collectives: 13.2 us -> none  [on_device(): var_cot = lax.all_gather(cotangent, 'mem', axis=0, tiled=True)]
    reshape x0 -> x6, local copies, waits for them, and re-layouts: none -> 10.8 us  [the longest x2 4.06 us: on_device(): packed = alpha.reshape(modes, members, tiles, chunks, width)]
    dot_general x2 -> x0, matrix products: 9.86 us -> none  [the longest x1 5.67 us: lift_control(): jnp.einsum('lm,mkg->klg', vert_root, modes_all, preferred_element_type=jn...]
  transfers between devices with their start and end apart: 5 -> 0, of which waited for: 5 -> 0; matrix products, arithmetic and copies ran while one was open for 11% -> 0% of each run, Pallas kernels for 0% -> 0%
where the time goes in v1:
time: 83.2 us; the launch traced here: 82.9 us
  Pallas kernels  68.9 us (83%)
  local copies, waits for them, and re-layouts  13.3 us (16%)
    pallas_call x1, Pallas kernels, on_device(): pl.pallas_call(functools.partial(kernel, scale, tiles, levels), out_shape...  68.9 us
    reshape x2, local copies, waits for them, and re-layouts, on_device(): packed = alpha.reshape(modes, members, tiles, chunks, width)  4.06 us
    reshape x1, local copies, waits for them, and re-layouts, on_device(): grad.reshape(chunks, modes, members, tiles, width).transpose(1, 2, 3, 0, 4)  2.62 us
    reshape x1, local copies, waits for them, and re-layouts, on_device(): return (increment[None], grad.reshape(modes, members, whole))  2.06 us
    unnamed x4, local copies, waits for them, and re-layouts  1.81 us

profile of v1, /device:TPU:0, one launch (start us, length us, event | category | flops | bytes accessed | tf_op | source)
XLA Modules:
  0.0 82.9 jit_solution(17285280691054090031)
XLA Ops:
  0.6 1.1 %copy.11 = bf16[2,8,8,1024]{3,2,1,0:T(8,128)(2,1)S(1)} copy(bf16[2,8,8,1024]{3,1,2,0:T(8,128)(2,1)} %bitcast.17) | data formatting | bytes 524288
  1.7 0.9 %copy.15 = bf16[16,8,1024]{2,0,1:T(8,128)(2,1)} copy(bf16[16,8,1024]{2,1,0:T(8,128)(2,1)S(1)} %bitcast.16) | data formatting | bytes 524288 | tf_op jit(solution)/shard_map/reshape | solution.py:271
  2.6 3.0 %reshape.19 = bf16[5,4,4,8,1024]{4,3,2,1,0:T(8,128)(2,1)S(1)} reshape(bf16[5,4,32768]{2,1,0:T(4,128)(2,1)} %param.5) | data formatting | bytes 2621440 | tf_op jit(solution)/shard_map/reshape | solution.py:269
  5.6 1.0 %copy.14 = bf16[5,4,4,8,1024]{4,2,1,0,3:T(4,128)(2,1)S(1)} copy(bf16[5,4,4,8,1024]{4,3,2,1,0:T(8,128)(2,1)S(1)} %reshape.19) | data formatting | bytes 2621440 | tf_op jit(solution)/shard_map/reshape | solution.py:269
  6.7 1.2 %reshape.20.alpha_ref = bf16[8,80,1024]{2,1,0:T(8,128)(2,1)} reshape(bf16[8,5,4,4,1024]{4,3,2,1,0:T(4,128)(2,1)S(1)} %bitcast.13) | data formatting | bytes 2621440 | tf_op jit(solution)/shard_map/reshape | solution.py:270
  7.9 68.9 %shard_map.59 = (bf16[16,8192]{1,0:T(8,128)(2,1)}, bf16[8,80,1024]{2,1,0:T(8,128)(2,1)}) custom-call(bf16[4,2,16,32768]{3,2,1,0:T(8,128)(2,1)} %ens_ref.1, bf16[8,80,1024]{2,1,0:T(8,128)(2,1)} %reshape.20.alpha_ref, bf16[16,20]{1,0:T(8,128)(2,1)} %root_ref.1, bf16[8,16,1024]{2,1,0:T(8,128)(2,1)} %bitcast.15), custom_call_target="tpu_custom_call" | custom-call | tf_op jit(solution)/shard_map/pallas_call | solution.py:274
  76.8 2.6 %reshape.22 = bf16[8,5,4,4,1024]{4,3,2,1,0:T(4,128)(2,1)S(1)} reshape(bf16[8,80,1024]{2,1,0:T(8,128)(2,1)} %get-tuple-element.5) | data formatting | bytes 2621440 | tf_op jit(solution)/shard_map/reshape | solution.py:326
  79.4 0.7 copy.10
  80.2 0.0 copy-start
  80.2 2.1 %reshape.23 = bf16[5,4,32768]{2,1,0:T(4,128)(2,1)} reshape(bf16[5,4,4,8,1024]{4,3,2,1,0:T(8,128)(2,1)S(1)} %copy.10) | data formatting | bytes 2621440 | tf_op jit(solution)/shard_map/reshape | solution.py:327
  82.2 0.0 copy-done
  82.2 0.7 copy.17
Async XLA Ops:
  80.2 2.1 %copy-start = (bf16[16,8192]{1,0:T(8,128)(2,1)S(1)}, bf16[16,8192]{1,0:T(8,128)(2,1)}, u32[]{:S(2)}) copy-start(bf16[16,8192]{1,0:T(8,128)(2,1)} %get-tuple-element.4) | copy-start | bytes 786436

commit v2 on v1

--- a/solution.py
+++ b/solution.py
@@ -22,11 +22,10 @@
 def kernel(scale, tiles, levels, ens_ref, alpha_ref, root_ref, cot_ref, inc_ref, grad_ref,
            ens, alpha, cot, lift_w, back_w, keep_c, keep_own, keep_y,
            c1s, c1r, c2s, c2r, d1s, d1r, d2s, d2r,
-           ens_sem, own_sem, cot_sem, a_ss, a_rs, bt_ss, bt_rs, bm_ss, bm_rs,
+           ens_sem, cot_sem, a_ss, a_rs, bt_ss, bt_rs, bm_ss, bm_rs,
            c1_ss, c1_rs, c2_ss, c2_rs, d1_ss, d1_rs, d2_ss, d2_rs):
-    chunks, rows, width = alpha_ref.shape
-    members = ens_ref.shape[0]
-    modes = root_ref.shape[1] // 4
+    chunks, _, rows, width = alpha.shape
+    modes, members, _ = alpha_ref.shape
     pairs = members * tiles
     cells = chunks * width
     mem, tile, lev = lax.axis_index("mem"), lax.axis_index("tile"), lax.axis_index("lev")
@@ -42,25 +41,30 @@
         )
 
     def a_far(c):
-        return remote(alpha_ref.at[c], alpha.at[c, 2], a_ss.at[c, 0], a_rs.at[c, 0], far)
+        return remote(alpha.at[c, 0], alpha.at[c, 2], a_ss.at[c, 0], a_rs.at[c, 0], far)
 
     def a_near(c):
-        return remote(alpha_ref.at[c], alpha.at[c, 1], a_ss.at[c, 1], a_rs.at[c, 1], near)
+        return remote(alpha.at[c, 0], alpha.at[c, 1], a_ss.at[c, 1], a_rs.at[c, 1], near)
 
     def a_pass(c):
         return remote(alpha.at[c, 2], alpha.at[c, 3], a_ss.at[c, 2], a_rs.at[c, 2], near)
 
-    def a_own(c):
-        return pltpu.make_async_copy(alpha_ref.at[c], alpha.at[c, 0], own_sem.at[c])
+    def place(c, t):
+        return pl.ds(pl.multiple_of(t * cells + c * width, width), width)
+
+    def pack(c):
+        for m in range(modes):
+            pieces = [alpha_ref[m, :, place(c, t)].astype(F32) for t in range(tiles)]
+            alpha[c, 0, m * pairs : (m + 1) * pairs, :] = jnp.concatenate(pieces, axis=0).astype(BF16)
 
     def b_own(c):
-        return pltpu.make_async_copy(cot_ref.at[c], cot.at[c, 0, tile], cot_sem.at[c])
+        return pltpu.make_async_copy(cot_ref.at[:, place(c, 0)], cot.at[c, 0, tile], cot_sem.at[c])
 
     def b_tile(c, i):
-        return remote(cot_ref.at[c], cot.at[c, 0, tile], bt_ss.at[c, i], bt_rs.at[c, i], tile_to[i])
+        return remote(cot_ref.at[:, place(c, 0)], cot.at[c, 0, tile], bt_ss.at[c, i], bt_rs.at[c, i], tile_to[i])
 
     def b_twin(c, i):
-        src = cot_ref.at[c] if i == 0 else cot.at[c, 0, tile_from[i]]
+        src = cot_ref.at[:, place(c, 0)] if i == 0 else cot.at[c, 0, tile_from[i]]
         return remote(src, cot.at[c, 1, tile_from[i]], bm_ss.at[c, i], bm_rs.at[c, i], twin)
 
     def c_twin(c):
@@ -77,16 +81,16 @@
         return remote(d2s.at[c], d2r.at[c], d2_ss.at[c], d2_rs.at[c], far)
 
     def e_load(c, t):
-        src = ens_ref.at[:, :, :, pl.ds(pl.multiple_of(t * cells + c * width, width), width)]
+        src = ens_ref.at[:, :, :, place(c, t)]
         return pltpu.make_async_copy(src, ens.at[c % SLOTS, t], ens_sem.at[c % SLOTS, t])
 
     def first_sends(c):
-        a_far(c).start()
         for i in range(1, tiles):
             b_tile(c, i).start()
         b_twin(c, 0).start()
+        pack(c)
+        a_far(c).start()
         a_near(c).start()
-        a_own(c).start()
         b_own(c).start()
 
     barrier = pltpu.get_barrier_semaphore()
@@ -146,8 +150,8 @@
                         ens[e, t, k, mem, :, cols].astype(F32) * own[t]
                         + ens[e, t, k, 1 - mem, :, cols].astype(F32) * other[t]
                     ).astype(BF16)
+                    for t in range(tiles)
                     for k in range(members)
-                    for t in range(tiles)
                 ],
                 axis=0,
             )
@@ -169,7 +173,7 @@
             for t in range(tiles):
                 own = other = None
                 for k in range(members):
-                    at = (k * tiles + t) * levels
+                    at = (t * members + k) * levels
                     part = lifted[at : at + levels]
                     one = ens[e, t, k, mem, :, cols].astype(F32) * part
                     two = ens[e, t, k, 1 - mem, :, cols].astype(F32) * part
@@ -209,7 +213,6 @@
                 b_twin(c, i).wait_recv()
             compute_adjoint(c)
             d_near(c).start()
-            a_own(c).wait()
             a_near(c).wait_recv()
             a_pass(c).wait_recv()
             compute_lift(c)
@@ -240,9 +243,14 @@
             for i in range(1, tiles):
                 c_tile(c, i).wait_recv()
                 total = total + c2r[c, i - 1].astype(F32)
-            inc_ref[:, pl.ds(pl.multiple_of(c * width, width), width)] = (total * scale).astype(BF16)
+            inc_ref[:, place(c, 0)] = (total * scale).astype(BF16)
             d_far(c).wait_recv()
-            grad_ref[c] = ((keep_own[slot] + d2r[c].astype(F32)) * scale).astype(BF16)
+            for m in range(modes):
+                at = slice(m * pairs, (m + 1) * pairs)
+                done = (keep_own[slot, at] + d2r[c, at].astype(F32)) * scale
+                for t in range(tiles):
+                    part = done[t * members : (t + 1) * members]
+                    grad_ref[m, :, place(c, t)] = part.astype(BF16)
 
     @pl.loop(0, chunks)
     def _(c):
@@ -266,20 +274,17 @@
     cells = whole // tiles
     chunks, width = CHUNKS, cells // CHUNKS
     rows = modes * members * tiles
-    packed = alpha.reshape(modes, members, tiles, chunks, width)
-    packed = packed.transpose(3, 0, 1, 2, 4).reshape(chunks, rows, width)
-    cot = cotangent.reshape(levels, chunks, width).transpose(1, 0, 2)
     vmem, dma = pltpu.VMEM, pltpu.SemaphoreType.DMA
     sums = (chunks, tiles, levels, width)
     increment, grad = pl.pallas_call(
         functools.partial(kernel, scale, tiles, levels),
         out_shape=(
             jax.ShapeDtypeStruct((levels, cells), BF16),
-            jax.ShapeDtypeStruct((chunks, rows, width), BF16),
+            jax.ShapeDtypeStruct(alpha.shape, BF16),
         ),
         in_specs=[
             pl.BlockSpec(memory_space=pl.ANY),
-            pl.BlockSpec(memory_space=pl.ANY),
+            pl.BlockSpec(memory_space=pltpu.VMEM),
             pl.BlockSpec(memory_space=pltpu.VMEM),
             pl.BlockSpec(memory_space=pl.ANY),
         ],
@@ -303,7 +308,6 @@
             vmem((chunks, rows, width), BF16),
             dma((SLOTS, tiles)),
             dma((chunks,)),
-            dma((chunks,)),
             dma((chunks, 3)),
             dma((chunks, 3)),
             dma((chunks, tiles)),
@@ -322,9 +326,8 @@
         compiler_params=pltpu.CompilerParams(
             collective_id=0, has_side_effects=True, vmem_limit_bytes=60 * 1024 * 1024
         ),
-    )(ensemble, packed, vert_root, cot)
-    grad = grad.reshape(chunks, modes, members, tiles, width).transpose(1, 2, 3, 0, 4)
-    return increment[None], grad.reshape(modes, members, whole)
+    )(ensemble, alpha, vert_root, cotangent.reshape(levels, cells))
+    return increment[None], grad
 
 
 def solution(mesh):

time: 83.2 us -> 74.6 us (0.90)
  local copies, waits for them, and re-layouts: 13.3 us -> 4.49 us
    reshape x6 -> x0, local copies, waits for them, and re-layouts: 10.8 us -> none  [the longest x2 4.06 us: on_device(): packed = alpha.reshape(modes, members, tiles, chunks, width)]
    unnamed x4 -> x2, local copies, waits for them, and re-layouts: 1.81 us -> 4.49 us
where the time goes in v2:
time: 74.6 us; the launch traced here: 74.4 us
  Pallas kernels  69.3 us (93%)
  local copies, waits for them, and re-layouts  4.49 us (6%)
    pallas_call x1, Pallas kernels, on_device(): pl.pallas_call(functools.partial(kernel, scale, tiles, levels), out_shape...  69.3 us
    unnamed x2, local copies, waits for them, and re-layouts  4.49 us

profile of v2, /device:TPU:0, one launch (start us, length us, event | category | flops | bytes accessed | tf_op | source)
XLA Modules:
  0.0 74.4 jit_solution(16527760853241806492)
XLA Ops:
  0.6 69.3 %shard_map.59 = (bf16[16,8192]{1,0:T(8,128)(2,1)}, bf16[5,4,32768]{2,1,0:T(4,128)(2,1)}) custom-call(bf16[4,2,16,32768]{3,2,1,0:T(8,128)(2,1)} %ens_ref.1, bf16[5,4,32768]{2,1,0:T(4,128)(2,1)} %alpha_ref.1, bf16[16,20]{1,0:T(8,128)(2,1)} %root_ref.1, bf16[16,8192]{1,0:T(8,128)(2,1)} %bitcast.2), custom_call_target="tpu_custom_call" | custom-call | tf_op jit(solution)/shard_map/pallas_call | solution.py:279
  69.9 1.7 %copy.8 = bf16[1,16,8192]{2,1,0:T(8,128)(2,1)} copy(bf16[1,16,8192]{2,1,0:T(8,128)(2,1)} %bitcast.3) | data formatting | bytes 524288
  71.6 2.8 %copy.9 = bf16[5,4,32768]{2,1,0:T(4,128)(2,1)} copy(bf16[5,4,32768]{2,1,0:T(4,128)(2,1)} %get-tuple-element.9) | data formatting | bytes 2621440
